TPU v7x, 512 devices: a whole 4x8x8 slice. The times are simulated.
512 devices in a mesh: chan: 16 (over x_lo, y), tm: 32 (over z, x_hi, core).
Axes of the slice: x: 4 (x_hi: 2, x_lo: 2; x = x_hi * 2 + x_lo), y: 8, z: 8, core: 2. Of those that a mesh axis runs over, the one named last changes fastest.
Arguments:
- samples: bfloat16 [1024, 262144], P('chan', 'tm'), may hold values from -6 to 6
- cell_of_feed: int32 [1024], replicated, may hold values from 0 to 1023, each once
Outputs:
- beam_power: float32 [32, 1024, 1024], P('tm', 'chan')
Inputs may be any that keep to these rules, and one draw needn't show every extreme that they name: `cell_of_feed`: each grid cell is named by exactly one feed.
All inputs are finite; a program needn't handle non-finite values.
Results may differ from a plain program's by a relative error of at most 0.0019.
Values may be sent and summed in bfloat16 or wider, within the bound.
A program may use at most 64 MiB of HBM per device.

v0:
```python
import functools
import math

import jax
import jax.numpy as jnp
import ml_dtypes
import numpy as np
from jax import lax
from jax.experimental import pallas as pl
from jax.experimental.pallas import tpu as pltpu
from jax.sharding import PartitionSpec as P

POSN = 256
CYL = 4
NFFT = 2048
TAPS = 4
TSUM = 4
INPUTS = 1024

STEP = 16
FINE = NFFT // STEP
HALF = FINE // 2
HISTORY = TAPS - 1

BF16 = jnp.bfloat16
F32 = jnp.float32
MESH = pl.DeviceIdType.MESH


def two_parts(table):
    high = table.astype(ml_dtypes.bfloat16)
    low = (table - high.astype(np.float64)).astype(ml_dtypes.bfloat16)
    return np.stack([high, low])


def window_table():
    offsets = np.arange(TAPS * NFFT) + 0.5
    shaped = np.sinc(offsets / NFFT - TAPS / 2.0)
    tapered = 0.5 - 0.5 * np.cos(offsets * (2.0 * math.pi / (TAPS * NFFT)))
    return (shaped * tapered).reshape(TAPS, NFFT).astype(np.float32)


def channel_tables():
    b = np.arange(FINE)[:, None]
    j = np.arange(HALF)[None, :]

    def waves(s):
        angle = 2.0 * math.pi * ((b * (STEP * j + s)) % NFFT) / NFFT
        return np.cos(angle), np.sin(angle)

    out = np.zeros((STEP // 2, 2 * FINE, 2 * FINE))
    for half, s in enumerate((0, STEP // 2)):
        cos, sin = waves(s)
        out[0, half * FINE : (half + 1) * FINE, half * FINE : (half + 1) * FINE] = np.concatenate([cos, -sin], 1)
    for p in range(1, STEP // 2):
        cos, sin = waves(p)
        out[p, :FINE, :FINE] = np.concatenate([cos, -sin], 1)
        out[p, FINE:, :FINE] = np.concatenate([sin, cos], 1)
        cos, sin = waves(STEP - p)
        out[p, :FINE, FINE:] = np.concatenate([cos, -sin], 1)
        out[p, FINE:, FINE:] = np.concatenate([-sin, -cos], 1)
    return two_parts(out / math.sqrt(NFFT))


def position_tables():
    v = np.arange(POSN)
    angle = 2.0 * math.pi * ((v[:, None] * v[None, :]) % POSN) / POSN
    return two_parts(np.concatenate([np.cos(angle), np.sin(angle)], 1))


def short_dft(x):
    c1, c2, c3 = (math.cos(math.pi * n / 8) for n in (1, 2, 3))
    s = [x[a] + x[a + 8] for a in range(8)]
    d = [x[a] - x[a + 8] for a in range(8)]
    ss = [s[a] + s[a + 4] for a in range(4)]
    sd = [s[a] - s[a + 4] for a in range(4)]
    p0, p1 = ss[0] + ss[2], ss[1] + ss[3]
    t1, t2 = c2 * (sd[1] - sd[3]), c2 * (sd[1] + sd[3])
    f = [None] + [d[a] - d[8 - a] for a in (1, 2, 3)]
    g = [None] + [d[a] + d[8 - a] for a in (1, 2, 3)]
    cf, cg = c2 * f[2], c2 * g[2]
    even, odd = d[0] + cf, d[0] - cf
    pp, qq = c1 * f[1] + c3 * f[3], c3 * f[1] - c1 * f[3]
    vv, ww = c3 * g[1] + c1 * g[3], c1 * g[1] - c3 * g[3]
    ee, ff = cg + d[4], cg - d[4]
    return [
        (p0 + p1, p0 - p1),
        (even + pp, -(vv + ee)),
        (sd[0] + t1, -(sd[2] + t2)),
        (odd + qq, -(ww + ff)),
        (ss[0] - ss[2], ss[3] - ss[1]),
        (odd - qq, ff - ww),
        (sd[0] - t1, sd[2] - t2),
        (even - pp, ee - vv),
    ]


def dot(left, right):
    return jnp.dot(left, right, preferred_element_type=F32)


def kernel(
    peers,
    blocks,
    samples,
    cell,
    window_in,
    channel_in,
    position_in,
    out,
    frames,
    window,
    channel,
    position,
    terms,
    outgoing,
    spectra,
    choose,
    along,
    energy,
    packed,
    arrived,
    ordered,
    load_sem,
    halo_send,
    halo_recv,
    spectra_send,
    spectra_recv,
    power_send,
    power_recv,
):
    me = lax.axis_index("chan")
    block = lax.axis_index("tm")
    after = lax.rem(block + 1, blocks)
    before = lax.rem(block + blocks - 1, blocks)

    def peer(k):
        return lax.rem(me + k, peers)

    barrier = pltpu.get_barrier_semaphore()
    pl.semaphore_signal(barrier, inc=1, device_id={"tm": before}, device_id_type=MESH)

    def greet(k, carry):
        pl.semaphore_signal(barrier, inc=1, device_id={"chan": peer(k)}, device_id_type=MESH)
        return carry

    lax.fori_loop(1, peers, greet, 0)

    loads = [
        pltpu.make_async_copy(samples.at[:, pl.ds(q * NFFT, NFFT)], frames.at[HISTORY + q], load_sem.at[q])
        for q in range(TSUM)
    ]
    loads.append(pltpu.make_async_copy(window_in, window, load_sem.at[4]))
    loads.append(pltpu.make_async_copy(channel_in, channel, load_sem.at[5]))
    loads.append(pltpu.make_async_copy(position_in, position, load_sem.at[6]))
    for load in loads:
        load.start()

    def halo(f):
        return pltpu.make_async_remote_copy(
            src_ref=samples.at[:, pl.ds((f + 1) * NFFT, NFFT)],
            dst_ref=frames.at[f],
            send_sem=halo_send.at[f],
            recv_sem=halo_recv.at[f],
            device_id={"tm": after},
            device_id_type=MESH,
        )

    def spectra_copy(t, source, target, k, slot):
        return pltpu.make_async_remote_copy(
            src_ref=outgoing.at[t, source],
            dst_ref=spectra.at[t, slot],
            send_sem=spectra_send.at[t, k],
            recv_sem=spectra_recv.at[t, slot],
            device_id={"chan": target},
            device_id_type=MESH,
        )

    def power_copy(source, target, k, slot):
        return pltpu.make_async_remote_copy(
            src_ref=packed.at[source],
            dst_ref=arrived.at[slot],
            send_sem=power_send.at[k],
            recv_sem=power_recv.at[slot],
            device_id={"chan": target},
            device_id_type=MESH,
        )

    def filter_frame(t):
        def rows_of(r, carry):
            rows = pl.ds(pl.multiple_of(r * 16, 16), 16)
            x = []
            for a in range(STEP):
                lanes = pl.ds(a * FINE, FINE)
                total = None
                for k in range(TAPS):
                    term = window[pl.ds(k, 1), lanes] * frames[t + k, rows, lanes].astype(F32)
                    total = term if total is None else total + term
                x.append(total)
            for p, pair in enumerate(short_dft(x)):
                for part, value in enumerate(pair):
                    lanes = pl.ds(part * FINE, FINE)
                    high = value.astype(BF16)
                    terms[p, rows, lanes] = high
                    terms[p, pl.ds(pl.multiple_of(64 + r * 16, 16), 16), lanes] = (value - high.astype(F32)).astype(BF16)
            return carry

        lax.fori_loop(0, 4, rows_of, 0)

    def channelize(t):
        for p in range(STEP // 2):
            first = dot(terms[p], channel[0, p])
            second = dot(terms[p, pl.ds(0, 64), :], channel[1, p])
            result = (first[:64] + first[64:] + second).astype(BF16)
            outgoing[t, p] = result[:, :FINE]
            outgoing[t, 8 if p == 0 else STEP - p] = result[:, FINE:]

    def send_spectra(t):
        def one(k, carry):
            spectra_copy(t, peer(k), peer(k), k, me).start()
            return carry

        lax.fori_loop(1, peers, one, 0)
        spectra[t, me] = outgoing[t, me]

    for load in loads[:6]:
        load.wait()
    filter_frame(TSUM - 1)
    channelize(TSUM - 1)
    pl.semaphore_wait(barrier, peers)
    for f in (2, 1, 0):
        halo(f).start()
    send_spectra(TSUM - 1)

    def choose_rows(r, carry):
        first = pl.multiple_of(r * 32, 32)
        number = lax.broadcasted_iota(jnp.int32, (32, INPUTS), 0) + first
        choose[pl.ds(first, 32), :] = jnp.where(number == cell[...], 1.0, 0.0).astype(BF16)
        return carry

    lax.fori_loop(0, INPUTS // 32, choose_rows, 0)

    def later_frame(step, carry):
        t = TSUM - 1 - step
        halo(t).wait_recv()

        @pl.when(block == 0)
        def _():
            frames[t] = jnp.zeros((64, NFFT), BF16)

        filter_frame(t)
        channelize(t)
        send_spectra(t)
        return carry

    lax.fori_loop(1, TSUM, later_frame, 0)

    loads[6].wait()
    lane = lax.broadcasted_iota(jnp.int32, (1, FINE), 1)
    left = lane < HALF
    sign = jnp.where(left, 1.0, -1.0)

    def turned(value):
        return pltpu.roll(value, HALF, 1) * sign

    def beams_of(pair, carry):
        for t in (2 * pair, 2 * pair + 1):

            def landed(k, inner, t=t):
                spectra_copy(t, me, me, k, peer(k)).wait_recv()
                return inner

            lax.fori_loop(1, peers, landed, 0)
        received = jnp.concatenate(
            [spectra[2 * pair + n].reshape(INPUTS, FINE) for n in range(2)], axis=1
        )
        for g in range(CYL):
            placed = dot(choose[pl.ds(g * POSN, POSN), :], received)
            swapped = jnp.concatenate([turned(placed[:, :FINE]), turned(placed[:, FINE:])], axis=1)
            both = jnp.concatenate([placed, swapped], axis=0).astype(BF16)
            along[g] = dot(position[0], both) + dot(position[1], both)

        def power_rows(r, inner):
            rows = pl.ds(pl.multiple_of(r * 16, 16), 16)
            squares = [None] * CYL
            for n in range(2):
                a = [along[g, rows, pl.ds(n * FINE, FINE)] for g in range(CYL)]
                even, odd = a[0] + a[2], a[1] + a[3]
                across, quarter = a[0] - a[2], turned(a[1] - a[3])
                for u, beam in enumerate((even + odd, across + quarter, even - odd, across - quarter)):
                    squares[u] = beam * beam if n == 0 else squares[u] + beam * beam
            for u in range(CYL):
                energy[u, rows, :] += squares[u]
            return inner

        lax.fori_loop(0, POSN // 16, power_rows, 0)
        return carry

    energy[...] = jnp.zeros_like(energy)
    beams_of(1, 0)
    beams_of(0, 0)

    for duo in range(2):
        for side in range(2):
            rows = pl.ds(side * 128, 128)
            one, two = energy[2 * duo, rows, :], energy[2 * duo + 1, rows, :]
            both = jnp.where(left, one, two) + pltpu.roll(jnp.where(left, two, one), HALF, 1)
            upright = (both * (1.0 / (TSUM * INPUTS))).T
            for u in range(2):
                low = upright[u * HALF : u * HALF + 32]
                high = upright[u * HALF + 32 : u * HALF + 64]
                target = (2 * duo + u) * 4 + 2 * side
                packed[target] = jnp.where(left, low, pltpu.roll(high, HALF, 1))
                packed[target + 1] = jnp.where(left, pltpu.roll(low, HALF, 1), high)

    def send_power(k, carry):
        power_copy(peer(k), peer(k), k, me).start()
        return carry

    lax.fori_loop(1, peers, send_power, 0)
    arrived[me] = packed[me]

    def settle(k, carry):
        for t in range(TSUM):
            spectra_copy(t, peer(k), peer(k), k, me).wait_send()
        power_copy(peer(k), peer(k), k, me).wait_send()
        return carry

    for f in range(HISTORY):
        halo(f).wait_send()
    lax.fori_loop(1, peers, settle, 0)

    def power_landed(k, carry):
        power_copy(me, me, k, peer(k)).wait_recv()
        return carry

    lax.fori_loop(1, peers, power_landed, 0)
    for s in range(STEP):
        ordered[pl.ds(s, 32, stride=STEP), :] = arrived[s]
    for q in range(4):
        upright = ordered[pl.ds(q * 128, 128), :].T
        out[:, pl.ds(q * 128, 128)] = upright[:HALF]
        out[:, pl.ds(512 + q * 128, 128)] = upright[HALF:]


def local(peers, blocks, samples, cell_of_feed):
    vmem = pl.BlockSpec(memory_space=pltpu.VMEM)
    anywhere = pl.BlockSpec(memory_space=pl.ANY)
    dma = pltpu.SemaphoreType.DMA
    power = pl.pallas_call(
        functools.partial(kernel, peers, blocks),
        out_shape=jax.ShapeDtypeStruct((64, 1024), F32),
        in_specs=[anywhere, vmem, anywhere, anywhere, anywhere],
        out_specs=vmem,
        scratch_shapes=[
            pltpu.VMEM((HISTORY + TSUM, 64, NFFT), BF16),
            pltpu.VMEM((TAPS, NFFT), F32),
            pltpu.VMEM((2, STEP // 2, 2 * FINE, 2 * FINE), BF16),
            pltpu.VMEM((2, POSN, 2 * POSN), BF16),
            pltpu.VMEM((STEP // 2, 128, 2 * FINE), BF16),
            pltpu.VMEM((TSUM, peers, 64, FINE), BF16),
            pltpu.VMEM((TSUM, peers, 64, FINE), BF16),
            pltpu.VMEM((INPUTS, INPUTS), BF16),
            pltpu.VMEM((CYL, POSN, 2 * FINE), F32),
            pltpu.VMEM((CYL, POSN, FINE), F32),
            pltpu.VMEM((peers, 32, 128), F32),
            pltpu.VMEM((peers, 32, 128), F32),
            pltpu.VMEM((512, 128), F32),
            dma((7,)),
            dma((HISTORY,)),
            dma((HISTORY,)),
            dma((TSUM, peers)),
            dma((TSUM, peers)),
            dma((peers,)),
            dma((peers,)),
        ],
        compiler_params=pltpu.CompilerParams(
            collective_id=0, has_side_effects=True, vmem_limit_bytes=60 * 1024 * 1024
        ),
    )(
        samples,
        cell_of_feed.reshape(1, INPUTS),
        jnp.asarray(window_table()),
        jnp.asarray(channel_tables()),
        jnp.asarray(position_tables()),
    )
    return power.reshape(1, 64, 1024)


def solution(mesh):
    return jax.shard_map(
        functools.partial(local, mesh.shape["chan"], mesh.shape["tm"]),
        mesh=mesh,
        in_specs=(P("chan", "tm"), P()),
        out_specs=P("tm", "chan", None),
        check_vma=False,
    )
```

profile of v0, /device:TPU:2, one launch (start us, length us, event | category | flops | bytes accessed | tf_op | source)
XLA Modules:
  0.0 57.0 jit_solution(2726321929882007083)
XLA Ops:
  0.0 55.3 %shard_map.55 = f32[64,1024]{1,0:T(8,128)} custom-call(bf16[64,8192]{1,0:T(8,128)(2,1)} %samples.1, s32[1,1024]{1,0:T(1,128)} %bitcast.3, f32[4,2048]{1,0:T(4,128)} %constant.6.clone.window_in, bf16[2,8,256,256]{3,2,1,0:T(8,128)(2,1)} %constant.7.clone.channel_in, bf16[2,256,512]{2,1,0:T(8,128)(2,1)} %constant.8.clone.position_in), custom_call_target="tpu_custom_call" | custom-call | tf_op jit(solution)/shard_map/pallas_call | solution.py:350
  55.3 1.7 %copy.7 = f32[1,64,1024]{2,1,0:T(8,128)} copy(f32[1,64,1024]{2,1,0:T(8,128)} %bitcast.2) | data formatting | bytes 524288
where the time goes:
time: 57.2 us; the launch traced here: 57 us
  Pallas kernels  55.3 us (97%)
  local copies, waits for them, and re-layouts  1.67 us (3%)
    pallas_call x1, Pallas kernels, local(): pl.pallas_call(functools.partial(kernel, peers, blocks), out_shape=jax.Sh...  55.3 us
    unnamed x1, local copies, waits for them, and re-layouts  1.67 us

commit v1 on v0

--- a/solution.py
+++ b/solution.py
@@ -103,12 +103,14 @@
     peers,
     blocks,
     samples,
-    cell,
+    cell_in,
     window_in,
     channel_in,
     position_in,
-    out,
+    arrived,
+    scale_in,
     frames,
+    cell,
     window,
     channel,
     position,
@@ -119,8 +121,7 @@
     along,
     energy,
     packed,
-    arrived,
-    ordered,
+    scale_out,
     load_sem,
     halo_send,
     halo_recv,
@@ -128,17 +129,24 @@
     spectra_recv,
     power_send,
     power_recv,
+    scale_send,
+    scale_recv,
 ):
     me = lax.axis_index("chan")
     block = lax.axis_index("tm")
-    after = lax.rem(block + 1, blocks)
-    before = lax.rem(block + blocks - 1, blocks)
+    is_first, is_last = block == 0, block == blocks - 1
 
     def peer(k):
         return lax.rem(me + k, peers)
 
+    def drained(ref, sem):
+        pltpu.make_async_copy(ref, ref, sem).wait()
+
     barrier = pltpu.get_barrier_semaphore()
-    pl.semaphore_signal(barrier, inc=1, device_id={"tm": before}, device_id_type=MESH)
+
+    @pl.when(jnp.logical_not(is_first))
+    def _():
+        pl.semaphore_signal(barrier, inc=1, device_id={"tm": block - 1}, device_id_type=MESH)
 
     def greet(k, carry):
         pl.semaphore_signal(barrier, inc=1, device_id={"chan": peer(k)}, device_id_type=MESH)
@@ -146,13 +154,16 @@
 
     lax.fori_loop(1, peers, greet, 0)
 
+    for q in range(TSUM):
+        pltpu.make_async_copy(
+            samples.at[:, pl.ds(q * NFFT, NFFT)], frames.at[HISTORY + q], load_sem.at[0]
+        ).start()
     loads = [
-        pltpu.make_async_copy(samples.at[:, pl.ds(q * NFFT, NFFT)], frames.at[HISTORY + q], load_sem.at[q])
-        for q in range(TSUM)
+        pltpu.make_async_copy(source, target, load_sem.at[n + 1])
+        for n, (source, target) in enumerate(
+            ((window_in, window), (channel_in, channel), (position_in, position), (cell_in, cell))
+        )
     ]
-    loads.append(pltpu.make_async_copy(window_in, window, load_sem.at[4]))
-    loads.append(pltpu.make_async_copy(channel_in, channel, load_sem.at[5]))
-    loads.append(pltpu.make_async_copy(position_in, position, load_sem.at[6]))
     for load in loads:
         load.start()
 
@@ -160,28 +171,38 @@
         return pltpu.make_async_remote_copy(
             src_ref=samples.at[:, pl.ds((f + 1) * NFFT, NFFT)],
             dst_ref=frames.at[f],
-            send_sem=halo_send.at[f],
+            send_sem=halo_send,
             recv_sem=halo_recv.at[f],
-            device_id={"tm": after},
+            device_id={"tm": block + 1},
             device_id_type=MESH,
         )
 
-    def spectra_copy(t, source, target, k, slot):
+    def spectra_copy(t, target):
         return pltpu.make_async_remote_copy(
-            src_ref=outgoing.at[t, source],
-            dst_ref=spectra.at[t, slot],
-            send_sem=spectra_send.at[t, k],
-            recv_sem=spectra_recv.at[t, slot],
+            src_ref=outgoing.at[t, target],
+            dst_ref=spectra.at[t, me],
+            send_sem=spectra_send,
+            recv_sem=spectra_recv.at[t],
             device_id={"chan": target},
             device_id_type=MESH,
         )
 
-    def power_copy(source, target, k, slot):
+    def power_copy(target):
         return pltpu.make_async_remote_copy(
-            src_ref=packed.at[source],
-            dst_ref=arrived.at[slot],
-            send_sem=power_send.at[k],
-            recv_sem=power_recv.at[slot],
+            src_ref=packed.at[target],
+            dst_ref=arrived.at[me],
+            send_sem=power_send,
+            recv_sem=power_recv,
+            device_id={"chan": target},
+            device_id_type=MESH,
+        )
+
+    def scale_copy(target):
+        return pltpu.make_async_remote_copy(
+            src_ref=scale_out.at[target],
+            dst_ref=scale_in.at[me],
+            send_sem=scale_send,
+            recv_sem=scale_recv,
             device_id={"chan": target},
             device_id_type=MESH,
         )
@@ -217,20 +238,27 @@
 
     def send_spectra(t):
         def one(k, carry):
-            spectra_copy(t, peer(k), peer(k), k, me).start()
+            spectra_copy(t, peer(k)).start()
             return carry
 
         lax.fori_loop(1, peers, one, 0)
         spectra[t, me] = outgoing[t, me]
 
-    for load in loads[:6]:
-        load.wait()
+    drained(frames.at[pl.ds(HISTORY, TSUM)], load_sem.at[0])
+    loads[0].wait()
     filter_frame(TSUM - 1)
+    loads[1].wait()
     channelize(TSUM - 1)
-    pl.semaphore_wait(barrier, peers)
-    for f in (2, 1, 0):
-        halo(f).start()
+    pl.semaphore_wait(barrier, jnp.where(is_last, peers - 1, peers))
+
+    @pl.when(jnp.logical_not(is_last))
+    def _():
+        for f in (2, 1, 0):
+            halo(f).start()
+
     send_spectra(TSUM - 1)
+
+    loads[3].wait()
 
     def choose_rows(r, carry):
         first = pl.multiple_of(r * 32, 32)
@@ -242,9 +270,12 @@
 
     def later_frame(step, carry):
         t = TSUM - 1 - step
-        halo(t).wait_recv()
-
-        @pl.when(block == 0)
+
+        @pl.when(jnp.logical_not(is_first))
+        def _():
+            halo(t).wait_recv()
+
+        @pl.when(is_first)
         def _():
             frames[t] = jnp.zeros((64, NFFT), BF16)
 
@@ -255,7 +286,7 @@
 
     lax.fori_loop(1, TSUM, later_frame, 0)
 
-    loads[6].wait()
+    loads[2].wait()
     lane = lax.broadcasted_iota(jnp.int32, (1, FINE), 1)
     left = lane < HALF
     sign = jnp.where(left, 1.0, -1.0)
@@ -263,80 +294,80 @@
     def turned(value):
         return pltpu.roll(value, HALF, 1) * sign
 
-    def beams_of(pair, carry):
-        for t in (2 * pair, 2 * pair + 1):
-
-            def landed(k, inner, t=t):
-                spectra_copy(t, me, me, k, peer(k)).wait_recv()
-                return inner
-
-            lax.fori_loop(1, peers, landed, 0)
-        received = jnp.concatenate(
-            [spectra[2 * pair + n].reshape(INPUTS, FINE) for n in range(2)], axis=1
-        )
+    def beams_of(t):
+        drained(spectra.at[t, pl.ds(0, peers - 1)], spectra_recv.at[t])
+        received = spectra[t].reshape(INPUTS, FINE)
         for g in range(CYL):
             placed = dot(choose[pl.ds(g * POSN, POSN), :], received)
-            swapped = jnp.concatenate([turned(placed[:, :FINE]), turned(placed[:, FINE:])], axis=1)
-            both = jnp.concatenate([placed, swapped], axis=0).astype(BF16)
+            both = jnp.concatenate([placed, turned(placed)], axis=0).astype(BF16)
             along[g] = dot(position[0], both) + dot(position[1], both)
 
-        def power_rows(r, inner):
-            rows = pl.ds(pl.multiple_of(r * 16, 16), 16)
-            squares = [None] * CYL
-            for n in range(2):
-                a = [along[g, rows, pl.ds(n * FINE, FINE)] for g in range(CYL)]
-                even, odd = a[0] + a[2], a[1] + a[3]
-                across, quarter = a[0] - a[2], turned(a[1] - a[3])
-                for u, beam in enumerate((even + odd, across + quarter, even - odd, across - quarter)):
-                    squares[u] = beam * beam if n == 0 else squares[u] + beam * beam
-            for u in range(CYL):
-                energy[u, rows, :] += squares[u]
-            return inner
-
-        lax.fori_loop(0, POSN // 16, power_rows, 0)
+    def power_of(first):
+        def power_rows(r, carry):
+            rows = pl.ds(pl.multiple_of(r * 32, 32), 32)
+            a = [along[g, rows, :] for g in range(CYL)]
+            even, odd = a[0] + a[2], a[1] + a[3]
+            across, quarter = a[0] - a[2], turned(a[1] - a[3])
+            squares = [beam * beam for beam in (even + odd, across + quarter, even - odd, across - quarter)]
+            for duo in range(2):
+                one, two = squares[2 * duo], squares[2 * duo + 1]
+                folded = jnp.where(left, one, two) + pltpu.roll(jnp.where(left, two, one), HALF, 1)
+                energy[duo, rows, :] = folded if first else energy[duo, rows, :] + folded
+            return carry
+
+        lax.fori_loop(0, POSN // 32, power_rows, 0, unroll=2)
+
+    beams_of(TSUM - 1)
+    power_of(True)
+
+    def more_beams(step, carry):
+        beams_of(TSUM - 1 - step)
+        power_of(False)
         return carry
 
-    energy[...] = jnp.zeros_like(energy)
-    beams_of(1, 0)
-    beams_of(0, 0)
+    lax.fori_loop(1, TSUM, more_beams, 0)
+
+    largest = jnp.max(jnp.max(jnp.maximum(energy[0], energy[1]), axis=0, keepdims=True), axis=1, keepdims=True)
+    largest = jnp.maximum(largest, 1e-36)
+    scale_out[...] = jnp.broadcast_to((largest * (1.0 / (TSUM * INPUTS))).reshape(1, 1, 1), (peers, 1, 128))
+    inverse = 1.0 / largest
 
     for duo in range(2):
         for side in range(2):
-            rows = pl.ds(side * 128, 128)
-            one, two = energy[2 * duo, rows, :], energy[2 * duo + 1, rows, :]
-            both = jnp.where(left, one, two) + pltpu.roll(jnp.where(left, two, one), HALF, 1)
-            upright = (both * (1.0 / (TSUM * INPUTS))).T
+            share = energy[duo, pl.ds(side * 128, 128), :] * inverse
+            share = share * share
+            upright = (share * share).T
             for u in range(2):
                 low = upright[u * HALF : u * HALF + 32]
                 high = upright[u * HALF + 32 : u * HALF + 64]
                 target = (2 * duo + u) * 4 + 2 * side
-                packed[target] = jnp.where(left, low, pltpu.roll(high, HALF, 1))
-                packed[target + 1] = jnp.where(left, pltpu.roll(low, HALF, 1), high)
+                packed[target] = jnp.where(left, low, pltpu.roll(high, HALF, 1)).astype(BF16)
+                packed[target + 1] = jnp.where(left, pltpu.roll(low, HALF, 1), high).astype(BF16)
 
     def send_power(k, carry):
-        power_copy(peer(k), peer(k), k, me).start()
+        scale_copy(peer(k)).start()
+        power_copy(peer(k)).start()
         return carry
 
     lax.fori_loop(1, peers, send_power, 0)
     arrived[me] = packed[me]
-
-    def settle(k, carry):
-        for t in range(TSUM):
-            spectra_copy(t, peer(k), peer(k), k, me).wait_send()
-        power_copy(peer(k), peer(k), k, me).wait_send()
-        return carry
-
-    for f in range(HISTORY):
-        halo(f).wait_send()
-    lax.fori_loop(1, peers, settle, 0)
-
-    def power_landed(k, carry):
-        power_copy(me, me, k, peer(k)).wait_recv()
-        return carry
-
-    lax.fori_loop(1, peers, power_landed, 0)
+    scale_in[me] = scale_out[me]
+
+    @pl.when(jnp.logical_not(is_last))
+    def _():
+        drained(frames.at[pl.ds(0, HISTORY)], halo_send)
+
+    others = pl.ds(0, peers - 1)
+    drained(outgoing.at[:, others], spectra_send)
+    drained(packed.at[others], power_send)
+    drained(scale_out.at[others], scale_send)
+    drained(arrived.at[others], power_recv)
+    drained(scale_in.at[others], scale_recv)
+
+
+def interleave(arrived, scale, out, ordered):
     for s in range(STEP):
-        ordered[pl.ds(s, 32, stride=STEP), :] = arrived[s]
+        ordered[pl.ds(s, 32, stride=STEP), :] = lax.rsqrt(lax.rsqrt(arrived[s].astype(F32))) * scale[s]
     for q in range(4):
         upright = ordered[pl.ds(q * 128, 128), :].T
         out[:, pl.ds(q * 128, 128)] = upright[:HALF]
@@ -347,13 +378,17 @@
     vmem = pl.BlockSpec(memory_space=pltpu.VMEM)
     anywhere = pl.BlockSpec(memory_space=pl.ANY)
     dma = pltpu.SemaphoreType.DMA
-    power = pl.pallas_call(
+    arrived, scale = pl.pallas_call(
         functools.partial(kernel, peers, blocks),
-        out_shape=jax.ShapeDtypeStruct((64, 1024), F32),
-        in_specs=[anywhere, vmem, anywhere, anywhere, anywhere],
-        out_specs=vmem,
+        out_shape=(
+            pltpu.VMEM((peers, 32, 128), BF16),
+            pltpu.VMEM((peers, 1, 128), F32),
+        ),
+        in_specs=[anywhere] * 5,
+        out_specs=(vmem, vmem),
         scratch_shapes=[
             pltpu.VMEM((HISTORY + TSUM, 64, NFFT), BF16),
+            pltpu.VMEM((1, INPUTS), jnp.int32),
             pltpu.VMEM((TAPS, NFFT), F32),
             pltpu.VMEM((2, STEP // 2, 2 * FINE, 2 * FINE), BF16),
             pltpu.VMEM((2, POSN, 2 * POSN), BF16),
@@ -361,18 +396,19 @@
             pltpu.VMEM((TSUM, peers, 64, FINE), BF16),
             pltpu.VMEM((TSUM, peers, 64, FINE), BF16),
             pltpu.VMEM((INPUTS, INPUTS), BF16),
-            pltpu.VMEM((CYL, POSN, 2 * FINE), F32),
             pltpu.VMEM((CYL, POSN, FINE), F32),
-            pltpu.VMEM((peers, 32, 128), F32),
-            pltpu.VMEM((peers, 32, 128), F32),
-            pltpu.VMEM((512, 128), F32),
-            dma((7,)),
+            pltpu.VMEM((2, POSN, FINE), F32),
+            pltpu.VMEM((peers, 32, 128), BF16),
+            pltpu.VMEM((peers, 1, 128), F32),
+            dma((5,)),
+            dma(()),
             dma((HISTORY,)),
-            dma((HISTORY,)),
-            dma((TSUM, peers)),
-            dma((TSUM, peers)),
-            dma((peers,)),
-            dma((peers,)),
+            dma(()),
+            dma((TSUM,)),
+            dma(()),
+            dma(()),
+            dma(()),
+            dma(()),
         ],
         compiler_params=pltpu.CompilerParams(
             collective_id=0, has_side_effects=True, vmem_limit_bytes=60 * 1024 * 1024
@@ -384,6 +420,13 @@
         jnp.asarray(channel_tables()),
         jnp.asarray(position_tables()),
     )
+    power = pl.pallas_call(
+        interleave,
+        out_shape=jax.ShapeDtypeStruct((64, 1024), F32),
+        in_specs=[vmem, vmem],
+        out_specs=vmem,
+        scratch_shapes=[pltpu.VMEM((512, 128), F32)],
+    )(arrived, scale)
     return power.reshape(1, 64, 1024)
 
 

time: 57.2 us -> 46.6 us (0.81)
  the two profiles are of different devices: /device:TPU:2 before, /device:TPU:196 now
where the time goes in v1:
time: 46.6 us; the launch traced here: 46.4 us
  Pallas kernels  45.2 us (97%)
  local copies, waits for them, and re-layouts  1.23 us (3%)
    pallas_call x1, Pallas kernels, local(): pl.pallas_call(functools.partial(kernel, peers, blocks), out_shape=(pltpu...  43.4 us
    pallas_call x1, Pallas kernels, local(): pl.pallas_call(interleave, out_shape=jax.ShapeDtypeStruct((64, 1024), F32...  1.8 us
    unnamed x4, local copies, waits for them, and re-layouts  1.23 us

profile of v1, /device:TPU:196, one launch (start us, length us, event | category | flops | bytes accessed | tf_op | source)
XLA Modules:
  0.0 46.4 jit_solution(11967967906465052968)
XLA Ops:
  0.0 43.4 %shard_map.55 = (bf16[16,32,128]{2,1,0:T(8,128)(2,1)S(1)}, f32[16,1,128]{2,1,0:T(1,128)S(1)}) custom-call(bf16[64,8192]{1,0:T(8,128)(2,1)} %samples.1, s32[1,1024]{1,0:T(1,128)} %bitcast.2, f32[4,2048]{1,0:T(4,128)} %constant.6.clone.window_in, bf16[2,8,256,256]{3,2,1,0:T(8,128)(2,1)} %constant.7.clone.channel_in, bf16[2,256,512]{2,1,0:T(8,128)(2,1)} %constant.8.clone.position_in), custom_call_target="tpu_custom_call" | custom-call | tf_op jit(solution)/shard_map/pallas_call | solution.py:381
  43.4 0.0 copy-start
  43.4 0.6 %copy-done = bf16[16,32,128]{2,1,0:T(8,128)(2,1)} copy-done((bf16[16,32,128]{2,1,0:T(8,128)(2,1)}, bf16[16,32,128]{2,1,0:T(8,128)(2,1)S(1)}, u32[]{:S(2)}) %copy-start) | copy-done | bytes 131096
  44.0 0.0 copy-start.1
  44.0 0.6 %copy-done.1 = f32[16,1,128]{2,1,0:T(1,128)} copy-done((f32[16,1,128]{2,1,0:T(1,128)}, f32[16,1,128]{2,1,0:T(1,128)S(1)}, u32[]{:S(2)}) %copy-start.1) | copy-done | bytes 8216
  44.6 1.8 %shard_map.56 = f32[64,1024]{1,0:T(8,128)} custom-call(bf16[16,32,128]{2,1,0:T(8,128)(2,1)} %copy-done, f32[16,1,128]{2,1,0:T(1,128)} %copy-done.1), custom_call_target="tpu_custom_call" | custom-call | tf_op jit(solution)/shard_map/pallas_call | solution.py:423
Async XLA Ops:
  43.4 0.6 %copy-start = (bf16[16,32,128]{2,1,0:T(8,128)(2,1)}, bf16[16,32,128]{2,1,0:T(8,128)(2,1)S(1)}, u32[]{:S(2)}) copy-start(bf16[16,32,128]{2,1,0:T(8,128)(2,1)S(1)} %get-tuple-element.7.arrived) | copy-start | bytes 393220
  44.0 0.6 %copy-start.1 = (f32[16,1,128]{2,1,0:T(1,128)}, f32[16,1,128]{2,1,0:T(1,128)S(1)}, u32[]{:S(2)}) copy-start(f32[16,1,128]{2,1,0:T(1,128)S(1)} %get-tuple-element.8.scale) | copy-start | bytes 24580

commit v2 on v1

--- a/solution.py
+++ b/solution.py
@@ -63,9 +63,12 @@
 
 
 def position_tables():
-    v = np.arange(POSN)
-    angle = 2.0 * math.pi * ((v[:, None] * v[None, :]) % POSN) / POSN
-    return two_parts(np.concatenate([np.cos(angle), np.sin(angle)], 1))
+    v, r = np.arange(POSN // 2)[:, None], np.arange(POSN // 2)[None, :]
+    out = []
+    for odd in range(2):
+        angle = 2.0 * math.pi * ((v * (2 * r + odd)) % POSN) / POSN
+        out.append(np.concatenate(two_parts(np.concatenate([np.cos(angle), np.sin(angle)], 1))))
+    return np.stack(out)
 
 
 def short_dft(x):
@@ -131,13 +134,21 @@
     power_recv,
     scale_send,
     scale_recv,
+    around,
 ):
     me = lax.axis_index("chan")
     block = lax.axis_index("tm")
     is_first, is_last = block == 0, block == blocks - 1
 
-    def peer(k):
-        return lax.rem(me + k, peers)
+    def device(flip, dy):
+        return lax.rem(me // 8 + flip, 2) * 8 + lax.rem(lax.rem(me, 8) + 8 + dy, 8)
+
+    def near(k):
+        place = lax.rem(k + 2, 10)
+        return device(place // 5, lax.rem(place, 5) - 2)
+
+    def far(k):
+        return device(k // 3, lax.rem(k, 3) + 3)
 
     def drained(ref, sem):
         pltpu.make_async_copy(ref, ref, sem).wait()
@@ -149,10 +160,10 @@
         pl.semaphore_signal(barrier, inc=1, device_id={"tm": block - 1}, device_id_type=MESH)
 
     def greet(k, carry):
-        pl.semaphore_signal(barrier, inc=1, device_id={"chan": peer(k)}, device_id_type=MESH)
+        pl.semaphore_signal(barrier, inc=1, device_id={"chan": near(k)}, device_id_type=MESH)
         return carry
 
-    lax.fori_loop(1, peers, greet, 0)
+    lax.fori_loop(1, 10, greet, 0)
 
     for q in range(TSUM):
         pltpu.make_async_copy(
@@ -236,12 +247,19 @@
             outgoing[t, p] = result[:, :FINE]
             outgoing[t, 8 if p == 0 else STEP - p] = result[:, FINE:]
 
-    def send_spectra(t):
+    def send_near(t):
         def one(k, carry):
-            spectra_copy(t, peer(k)).start()
+            spectra_copy(t, near(k)).start()
             return carry
 
-        lax.fori_loop(1, peers, one, 0)
+        lax.fori_loop(1, 10, one, 0)
+
+    def send_far(t):
+        def one(k, carry):
+            spectra_copy(t, far(k)).start()
+            return carry
+
+        lax.fori_loop(0, 6, one, 0)
         spectra[t, me] = outgoing[t, me]
 
     drained(frames.at[pl.ds(HISTORY, TSUM)], load_sem.at[0])
@@ -249,20 +267,25 @@
     filter_frame(TSUM - 1)
     loads[1].wait()
     channelize(TSUM - 1)
-    pl.semaphore_wait(barrier, jnp.where(is_last, peers - 1, peers))
+    pl.semaphore_wait(barrier, jnp.where(is_last, 9, 10))
+    for dy in (2, 6):
+        pl.semaphore_signal(around, inc=1, device_id={"chan": device(0, dy)}, device_id_type=MESH)
 
     @pl.when(jnp.logical_not(is_last))
     def _():
         for f in (2, 1, 0):
             halo(f).start()
 
-    send_spectra(TSUM - 1)
+    send_near(TSUM - 1)
+    pl.semaphore_wait(around, 2)
+    send_far(TSUM - 1)
 
     loads[3].wait()
 
     def choose_rows(r, carry):
         first = pl.multiple_of(r * 32, 32)
-        number = lax.broadcasted_iota(jnp.int32, (32, INPUTS), 0) + first
+        base = first // POSN * POSN + lax.rem(first, POSN // 2) * 2 + lax.rem(first // (POSN // 2), 2)
+        number = lax.broadcasted_iota(jnp.int32, (32, INPUTS), 0) * 2 + base
         choose[pl.ds(first, 32), :] = jnp.where(number == cell[...], 1.0, 0.0).astype(BF16)
         return carry
 
@@ -281,7 +304,8 @@
 
         filter_frame(t)
         channelize(t)
-        send_spectra(t)
+        send_far(t)
+        send_near(t)
         return carry
 
     lax.fori_loop(1, TSUM, later_frame, 0)
@@ -294,21 +318,33 @@
     def turned(value):
         return pltpu.roll(value, HALF, 1) * sign
 
-    def beams_of(t):
-        drained(spectra.at[t, pl.ds(0, peers - 1)], spectra_recv.at[t])
-        received = spectra[t].reshape(INPUTS, FINE)
+    def beams_of(group):
+        for t in group:
+            drained(spectra.at[t, pl.ds(0, peers - 1)], spectra_recv.at[t])
+        received = jnp.concatenate([spectra[t].reshape(INPUTS, FINE) for t in group], axis=1)
+        half = POSN // 2
         for g in range(CYL):
             placed = dot(choose[pl.ds(g * POSN, POSN), :], received)
-            both = jnp.concatenate([placed, turned(placed)], axis=0).astype(BF16)
-            along[g] = dot(position[0], both) + dot(position[1], both)
-
-    def power_of(first):
+            swapped = jnp.concatenate([turned(placed[:, n * FINE : (n + 1) * FINE]) for n in range(len(group))], axis=1)
+            sums = []
+            for odd in range(2):
+                rows = slice(odd * half, (odd + 1) * half)
+                both = jnp.concatenate([placed[rows], swapped[rows]], axis=0).astype(BF16)
+                parts = dot(position[odd], both)
+                sums.append(parts[:half] + parts[half:])
+            along[g, :half, : len(group) * FINE] = sums[0] + sums[1]
+            along[g, half:, : len(group) * FINE] = sums[0] - sums[1]
+
+    def power_of(group, first):
         def power_rows(r, carry):
             rows = pl.ds(pl.multiple_of(r * 32, 32), 32)
-            a = [along[g, rows, :] for g in range(CYL)]
-            even, odd = a[0] + a[2], a[1] + a[3]
-            across, quarter = a[0] - a[2], turned(a[1] - a[3])
-            squares = [beam * beam for beam in (even + odd, across + quarter, even - odd, across - quarter)]
+            squares = [None] * CYL
+            for n in range(len(group)):
+                a = [along[g, rows, pl.ds(n * FINE, FINE)] for g in range(CYL)]
+                even, odd = a[0] + a[2], a[1] + a[3]
+                across, quarter = a[0] - a[2], turned(a[1] - a[3])
+                for u, beam in enumerate((even + odd, across + quarter, even - odd, across - quarter)):
+                    squares[u] = beam * beam if n == 0 else squares[u] + beam * beam
             for duo in range(2):
                 one, two = squares[2 * duo], squares[2 * duo + 1]
                 folded = jnp.where(left, one, two) + pltpu.roll(jnp.where(left, two, one), HALF, 1)
@@ -317,15 +353,9 @@
 
         lax.fori_loop(0, POSN // 32, power_rows, 0, unroll=2)
 
-    beams_of(TSUM - 1)
-    power_of(True)
-
-    def more_beams(step, carry):
-        beams_of(TSUM - 1 - step)
-        power_of(False)
-        return carry
-
-    lax.fori_loop(1, TSUM, more_beams, 0)
+    for n, group in enumerate(((3, 2), (1,), (0,))):
+        beams_of(group)
+        power_of(group, n == 0)
 
     largest = jnp.max(jnp.max(jnp.maximum(energy[0], energy[1]), axis=0, keepdims=True), axis=1, keepdims=True)
     largest = jnp.maximum(largest, 1e-36)
@@ -344,12 +374,20 @@
                 packed[target] = jnp.where(left, low, pltpu.roll(high, HALF, 1)).astype(BF16)
                 packed[target + 1] = jnp.where(left, pltpu.roll(low, HALF, 1), high).astype(BF16)
 
-    def send_power(k, carry):
-        scale_copy(peer(k)).start()
-        power_copy(peer(k)).start()
+    def send_power(target):
+        scale_copy(target).start()
+        power_copy(target).start()
+
+    def power_far(k, carry):
+        send_power(far(k))
         return carry
 
-    lax.fori_loop(1, peers, send_power, 0)
+    def power_near(k, carry):
+        send_power(near(k))
+        return carry
+
+    lax.fori_loop(0, 6, power_far, 0)
+    lax.fori_loop(1, 10, power_near, 0)
     arrived[me] = packed[me]
     scale_in[me] = scale_out[me]
 
@@ -391,12 +429,12 @@
             pltpu.VMEM((1, INPUTS), jnp.int32),
             pltpu.VMEM((TAPS, NFFT), F32),
             pltpu.VMEM((2, STEP // 2, 2 * FINE, 2 * FINE), BF16),
-            pltpu.VMEM((2, POSN, 2 * POSN), BF16),
+            pltpu.VMEM((2, POSN, POSN), BF16),
             pltpu.VMEM((STEP // 2, 128, 2 * FINE), BF16),
             pltpu.VMEM((TSUM, peers, 64, FINE), BF16),
             pltpu.VMEM((TSUM, peers, 64, FINE), BF16),
             pltpu.VMEM((INPUTS, INPUTS), BF16),
-            pltpu.VMEM((CYL, POSN, FINE), F32),
+            pltpu.VMEM((CYL, POSN, 2 * FINE), F32),
             pltpu.VMEM((2, POSN, FINE), F32),
             pltpu.VMEM((peers, 32, 128), BF16),
             pltpu.VMEM((peers, 1, 128), F32),
@@ -409,6 +447,7 @@
             dma(()),
             dma(()),
             dma(()),
+            pltpu.SemaphoreType.REGULAR,
         ],
         compiler_params=pltpu.CompilerParams(
             collective_id=0, has_side_effects=True, vmem_limit_bytes=60 * 1024 * 1024

time: 46.6 us -> 44 us (0.944)
  the two profiles are of different devices: /device:TPU:196 before, /device:TPU:1 now
where the time goes in v2:
time: 44 us; the launch traced here: 43.9 us
  Pallas kernels  42.7 us (97%)
  local copies, waits for them, and re-layouts  1.23 us (3%)
    pallas_call x1, Pallas kernels, local(): pl.pallas_call(functools.partial(kernel, peers, blocks), out_shape=(pltpu...  40.9 us
    pallas_call x1, Pallas kernels, local(): pl.pallas_call(interleave, out_shape=jax.ShapeDtypeStruct((64, 1024), F32...  1.8 us
    unnamed x4, local copies, waits for them, and re-layouts  1.23 us

profile of v2, /device:TPU:1, one launch (start us, length us, event | category | flops | bytes accessed | tf_op | source)
XLA Modules:
  0.0 43.9 jit_solution(7105686738617136873)
XLA Ops:
  0.0 40.9 %shard_map.55 = (bf16[16,32,128]{2,1,0:T(8,128)(2,1)S(1)}, f32[16,1,128]{2,1,0:T(1,128)S(1)}) custom-call(bf16[64,8192]{1,0:T(8,128)(2,1)} %samples.1, s32[1,1024]{1,0:T(1,128)} %bitcast.2, f32[4,2048]{1,0:T(4,128)} %constant.6.clone.window_in, bf16[2,8,256,256]{3,2,1,0:T(8,128)(2,1)} %constant.7.clone.channel_in, bf16[2,256,256]{2,1,0:T(8,128)(2,1)} %constant.8.clone.position_in), custom_call_target="tpu_custom_call" | custom-call | tf_op jit(solution)/shard_map/pallas_call | solution.py:419
  40.9 0.0 copy-start
  40.9 0.6 %copy-done = bf16[16,32,128]{2,1,0:T(8,128)(2,1)} copy-done((bf16[16,32,128]{2,1,0:T(8,128)(2,1)}, bf16[16,32,128]{2,1,0:T(8,128)(2,1)S(1)}, u32[]{:S(2)}) %copy-start) | copy-done | bytes 131096
  41.5 0.0 copy-start.1
  41.5 0.6 %copy-done.1 = f32[16,1,128]{2,1,0:T(1,128)} copy-done((f32[16,1,128]{2,1,0:T(1,128)}, f32[16,1,128]{2,1,0:T(1,128)S(1)}, u32[]{:S(2)}) %copy-start.1) | copy-done | bytes 8216
  42.1 1.8 %shard_map.56 = f32[64,1024]{1,0:T(8,128)} custom-call(bf16[16,32,128]{2,1,0:T(8,128)(2,1)} %copy-done, f32[16,1,128]{2,1,0:T(1,128)} %copy-done.1), custom_call_target="tpu_custom_call" | custom-call | tf_op jit(solution)/shard_map/pallas_call | solution.py:462
Async XLA Ops:
  40.9 0.6 %copy-start = (bf16[16,32,128]{2,1,0:T(8,128)(2,1)}, bf16[16,32,128]{2,1,0:T(8,128)(2,1)S(1)}, u32[]{:S(2)}) copy-start(bf16[16,32,128]{2,1,0:T(8,128)(2,1)S(1)} %get-tuple-element.7.arrived) | copy-start | bytes 393220
  41.5 0.6 %copy-start.1 = (f32[16,1,128]{2,1,0:T(1,128)}, f32[16,1,128]{2,1,0:T(1,128)S(1)}, u32[]{:S(2)}) copy-start(f32[16,1,128]{2,1,0:T(1,128)S(1)} %get-tuple-element.8.scale) | copy-start | bytes 24580

commit v3 on v2

--- a/solution.py
+++ b/solution.py
@@ -348,16 +348,18 @@
             for duo in range(2):
                 one, two = squares[2 * duo], squares[2 * duo + 1]
                 folded = jnp.where(left, one, two) + pltpu.roll(jnp.where(left, two, one), HALF, 1)
-                energy[duo, rows, :] = folded if first else energy[duo, rows, :] + folded
-            return carry
-
-        lax.fori_loop(0, POSN // 32, power_rows, 0, unroll=2)
+                folded = folded if first else energy[duo, rows, :] + folded
+                energy[duo, rows, :] = folded
+                carry = jnp.maximum(carry, jnp.max(folded.reshape(-1, 8, FINE), axis=0))
+            return carry
+
+        return lax.fori_loop(0, POSN // 32, power_rows, jnp.zeros((8, FINE), F32), unroll=4)
 
     for n, group in enumerate(((3, 2), (1,), (0,))):
         beams_of(group)
-        power_of(group, n == 0)
-
-    largest = jnp.max(jnp.max(jnp.maximum(energy[0], energy[1]), axis=0, keepdims=True), axis=1, keepdims=True)
+        heights = power_of(group, n == 0)
+
+    largest = jnp.max(jnp.max(heights, axis=0, keepdims=True), axis=1, keepdims=True)
     largest = jnp.maximum(largest, 1e-36)
     scale_out[...] = jnp.broadcast_to((largest * (1.0 / (TSUM * INPUTS))).reshape(1, 1, 1), (peers, 1, 128))
     inverse = 1.0 / largest
@@ -374,20 +376,20 @@
                 packed[target] = jnp.where(left, low, pltpu.roll(high, HALF, 1)).astype(BF16)
                 packed[target + 1] = jnp.where(left, pltpu.roll(low, HALF, 1), high).astype(BF16)
 
-    def send_power(target):
-        scale_copy(target).start()
-        power_copy(target).start()
-
-    def power_far(k, carry):
-        send_power(far(k))
-        return carry
-
-    def power_near(k, carry):
-        send_power(near(k))
-        return carry
-
-    lax.fori_loop(0, 6, power_far, 0)
-    lax.fori_loop(1, 10, power_near, 0)
+    def send_power(which, first, last):
+        def blocks_of(k, carry):
+            power_copy(which(k)).start()
+            return carry
+
+        def scales_of(k, carry):
+            scale_copy(which(k)).start()
+            return carry
+
+        lax.fori_loop(first, last, blocks_of, 0)
+        lax.fori_loop(first, last, scales_of, 0)
+
+    send_power(far, 0, 6)
+    send_power(near, 1, 10)
     arrived[me] = packed[me]
     scale_in[me] = scale_out[me]
 
@@ -403,13 +405,20 @@
     drained(scale_in.at[others], scale_recv)
 
 
-def interleave(arrived, scale, out, ordered):
-    for s in range(STEP):
-        ordered[pl.ds(s, 32, stride=STEP), :] = lax.rsqrt(lax.rsqrt(arrived[s].astype(F32))) * scale[s]
+def interleave(arrived, scale, out, ordered, ready, sem):
+    copies = []
     for q in range(4):
+        for s in range(STEP):
+            value = arrived[s, pl.ds(8 * q, 8), :].astype(F32)
+            ordered[pl.ds(q * 128 + s, 8, stride=STEP), :] = lax.rsqrt(lax.rsqrt(value)) * scale[s]
         upright = ordered[pl.ds(q * 128, 128), :].T
-        out[:, pl.ds(q * 128, 128)] = upright[:HALF]
-        out[:, pl.ds(512 + q * 128, 128)] = upright[HALF:]
+        for high in range(2):
+            lanes = pl.ds(512 * high + 128 * q, 128)
+            ready[:, lanes] = upright[HALF * high : HALF * (high + 1)]
+            copies.append(pltpu.make_async_copy(ready.at[:, lanes], out.at[:, lanes], sem.at[2 * q + high]))
+            copies[-1].start()
+    for copy in copies:
+        copy.wait()
 
 
 def local(peers, blocks, samples, cell_of_feed):
@@ -463,8 +472,9 @@
         interleave,
         out_shape=jax.ShapeDtypeStruct((64, 1024), F32),
         in_specs=[vmem, vmem],
-        out_specs=vmem,
-        scratch_shapes=[pltpu.VMEM((512, 128), F32)],
+        out_specs=anywhere,
+        scratch_shapes=[pltpu.VMEM((512, 128), F32), pltpu.VMEM((64, 1024), F32), dma((8,))],
+        compiler_params=pltpu.CompilerParams(vmem_limit_bytes=8 * 1024 * 1024),
     )(arrived, scale)
     return power.reshape(1, 64, 1024)
 

time: 44 us -> 41.6 us (0.945)
  Pallas kernels: 42.7 us -> 41.4 us
  local copies, waits for them, and re-layouts: 1.23 us -> 0 us
    unnamed x4 -> x0, local copies, waits for them, and re-layouts: 1.23 us -> none
    pallas_call x1, Pallas kernels: 1.8 us -> 0.91 us  [local(): pl.pallas_call(interleave, out_shape=jax.ShapeDtypeStruct((64, 1024), F32...]
where the time goes in v3:
time: 41.6 us; the launch traced here: 41.4 us
  Pallas kernels  41.4 us (100%)
    pallas_call x1, Pallas kernels, local(): pl.pallas_call(functools.partial(kernel, peers, blocks), out_shape=(pltpu...  40.5 us
    pallas_call x1, Pallas kernels, local(): pl.pallas_call(interleave, out_shape=jax.ShapeDtypeStruct((64, 1024), F32...  0.91 us

profile of v3, /device:TPU:1, one launch (start us, length us, event | category | flops | bytes accessed | tf_op | source)
XLA Modules:
  0.0 41.4 jit_solution(8023994614272610259)
XLA Ops:
  0.0 40.5 %shard_map.55 = (bf16[16,32,128]{2,1,0:T(8,128)(2,1)S(1)}, f32[16,1,128]{2,1,0:T(1,128)S(1)}) custom-call(bf16[64,8192]{1,0:T(8,128)(2,1)} %samples.1, s32[1,1024]{1,0:T(1,128)} %bitcast.2, f32[4,2048]{1,0:T(4,128)} %constant.6.clone.window_in, bf16[2,8,256,256]{3,2,1,0:T(8,128)(2,1)} %constant.7.clone.channel_in, bf16[2,256,256]{2,1,0:T(8,128)(2,1)} %constant.8.clone.position_in), custom_call_target="tpu_custom_call" | custom-call | tf_op jit(solution)/shard_map/pallas_call | solution.py:428
  40.5 0.9 %shard_map.56 = f32[64,1024]{1,0:T(8,128)} custom-call(bf16[16,32,128]{2,1,0:T(8,128)(2,1)S(1)} %get-tuple-element.7.arrived, f32[16,1,128]{2,1,0:T(1,128)S(1)} %get-tuple-element.8.scale), custom_call_target="tpu_custom_call" | custom-call | tf_op jit(solution)/shard_map/pallas_call | solution.py:471

commit v4 on v3

--- a/solution.py
+++ b/solution.py
@@ -408,9 +408,9 @@
 def interleave(arrived, scale, out, ordered, ready, sem):
     copies = []
     for q in range(4):
-        for s in range(STEP):
-            value = arrived[s, pl.ds(8 * q, 8), :].astype(F32)
-            ordered[pl.ds(q * 128 + s, 8, stride=STEP), :] = lax.rsqrt(lax.rsqrt(value)) * scale[s]
+        for s in range(STEP if q % 2 == 0 else 0):
+            value = arrived[s, pl.ds(8 * q, 16), :].astype(F32)
+            ordered[pl.ds(q * 128 + s, 16, stride=STEP), :] = lax.rsqrt(lax.rsqrt(value)) * scale[s]
         upright = ordered[pl.ds(q * 128, 128), :].T
         for high in range(2):
             lanes = pl.ds(512 * high + 128 * q, 128)

time: 41.6 us -> 41.6 us (level)
  no operation moved by 1% of the time
where the time goes in v4:
time: 41.6 us; the launch traced here: 41.4 us
  Pallas kernels  41.4 us (100%)
    pallas_call x1, Pallas kernels, local(): pl.pallas_call(functools.partial(kernel, peers, blocks), out_shape=(pltpu...  40.5 us
    pallas_call x1, Pallas kernels, local(): pl.pallas_call(interleave, out_shape=jax.ShapeDtypeStruct((64, 1024), F32...  0.91 us

profile of v4, /device:TPU:1, one launch (start us, length us, event | category | flops | bytes accessed | tf_op | source)
XLA Modules:
  0.0 41.4 jit_solution(8023994614272610259)
XLA Ops:
  0.0 40.5 %shard_map.55 = (bf16[16,32,128]{2,1,0:T(8,128)(2,1)S(1)}, f32[16,1,128]{2,1,0:T(1,128)S(1)}) custom-call(bf16[64,8192]{1,0:T(8,128)(2,1)} %samples.1, s32[1,1024]{1,0:T(1,128)} %bitcast.2, f32[4,2048]{1,0:T(4,128)} %constant.6.clone.window_in, bf16[2,8,256,256]{3,2,1,0:T(8,128)(2,1)} %constant.7.clone.channel_in, bf16[2,256,256]{2,1,0:T(8,128)(2,1)} %constant.8.clone.position_in), custom_call_target="tpu_custom_call" | custom-call | tf_op jit(solution)/shard_map/pallas_call | solution.py:428
  40.5 0.9 %shard_map.56 = f32[64,1024]{1,0:T(8,128)} custom-call(bf16[16,32,128]{2,1,0:T(8,128)(2,1)S(1)} %get-tuple-element.7.arrived, f32[16,1,128]{2,1,0:T(1,128)S(1)} %get-tuple-element.8.scale), custom_call_target="tpu_custom_call" | custom-call | tf_op jit(solution)/shard_map/pallas_call | solution.py:471

commit v5 on v4

--- a/solution.py
+++ b/solution.py
@@ -153,18 +153,6 @@
     def drained(ref, sem):
         pltpu.make_async_copy(ref, ref, sem).wait()
 
-    barrier = pltpu.get_barrier_semaphore()
-
-    @pl.when(jnp.logical_not(is_first))
-    def _():
-        pl.semaphore_signal(barrier, inc=1, device_id={"tm": block - 1}, device_id_type=MESH)
-
-    def greet(k, carry):
-        pl.semaphore_signal(barrier, inc=1, device_id={"chan": near(k)}, device_id_type=MESH)
-        return carry
-
-    lax.fori_loop(1, 10, greet, 0)
-
     for q in range(TSUM):
         pltpu.make_async_copy(
             samples.at[:, pl.ds(q * NFFT, NFFT)], frames.at[HISTORY + q], load_sem.at[0]
@@ -177,6 +165,18 @@
     ]
     for load in loads:
         load.start()
+
+    barrier = pltpu.get_barrier_semaphore()
+
+    @pl.when(jnp.logical_not(is_first))
+    def _():
+        pl.semaphore_signal(barrier, inc=1, device_id={"tm": block - 1}, device_id_type=MESH)
+
+    def greet(k, carry):
+        pl.semaphore_signal(barrier, inc=1, device_id={"chan": near(k)}, device_id_type=MESH)
+        return carry
+
+    lax.fori_loop(1, 10, greet, 0)
 
     def halo(f):
         return pltpu.make_async_remote_copy(
@@ -353,7 +353,7 @@
                 carry = jnp.maximum(carry, jnp.max(folded.reshape(-1, 8, FINE), axis=0))
             return carry
 
-        return lax.fori_loop(0, POSN // 32, power_rows, jnp.zeros((8, FINE), F32), unroll=4)
+        return lax.fori_loop(0, POSN // 32, power_rows, jnp.zeros((8, FINE), F32), unroll=8)
 
     for n, group in enumerate(((3, 2), (1,), (0,))):
         beams_of(group)

time: 41.6 us -> 41.9 us (level)
  no operation moved by 1% of the time
where the time goes in v5:
time: 41.9 us; the launch traced here: 41.7 us
  Pallas kernels  41.7 us (100%)
    pallas_call x1, Pallas kernels, local(): pl.pallas_call(functools.partial(kernel, peers, blocks), out_shape=(pltpu...  40.8 us
    pallas_call x1, Pallas kernels, local(): pl.pallas_call(interleave, out_shape=jax.ShapeDtypeStruct((64, 1024), F32...  0.91 us

profile of v5, /device:TPU:1, one launch (start us, length us, event | category | flops | bytes accessed | tf_op | source)
XLA Modules:
  0.0 41.7 jit_solution(11609681948456144568)
XLA Ops:
  0.0 40.8 %shard_map.55 = (bf16[16,32,128]{2,1,0:T(8,128)(2,1)S(1)}, f32[16,1,128]{2,1,0:T(1,128)S(1)}) custom-call(bf16[64,8192]{1,0:T(8,128)(2,1)} %samples.1, s32[1,1024]{1,0:T(1,128)} %bitcast.2, f32[4,2048]{1,0:T(4,128)} %constant.6.clone.window_in, bf16[2,8,256,256]{3,2,1,0:T(8,128)(2,1)} %constant.7.clone.channel_in, bf16[2,256,256]{2,1,0:T(8,128)(2,1)} %constant.8.clone.position_in), custom_call_target="tpu_custom_call" | custom-call | tf_op jit(solution)/shard_map/pallas_call | solution.py:428
  40.8 0.9 %shard_map.56 = f32[64,1024]{1,0:T(8,128)} custom-call(bf16[16,32,128]{2,1,0:T(8,128)(2,1)S(1)} %get-tuple-element.7.arrived, f32[16,1,128]{2,1,0:T(1,128)S(1)} %get-tuple-element.8.scale), custom_call_target="tpu_custom_call" | custom-call | tf_op jit(solution)/shard_map/pallas_call | solution.py:471
